TPU v7x, 32 devices: a whole 2x2x4 slice. The times are simulated.
32 devices in a mesh: blk: 8 (over y, x, core), grp: 4 (over z).
Axes of the slice: x: 2, y: 2, z: 4, core: 2. Of those that a mesh axis runs over, the one named last changes fastest.
Arguments:
- queries: bfloat16 [8, 640, 3072], P('blk', 'grp'), may hold values from -200 to 200
- keys: bfloat16 [8, 640, 3072], P('blk', 'grp'), may hold values from -6 to 6
- values: bfloat16 [8, 640, 3072], P('blk', 'grp'), may hold values from -6 to 6
- head_kind: int32 [24], replicated, may hold values from 0 to 1, as said below
- frame_reach: int32 [24], replicated, may hold values from 1 to 7
Outputs:
- attended: bfloat16 [8, 640, 3072], P('blk', 'grp')
Inputs may be any that keep to these rules, and one draw needn't show every extreme that they name: `head_kind`: exactly 16 of the 24 heads are 0, the others are 1.
All inputs are finite; a program needn't handle non-finite values.
Results may differ from a plain program's by a relative error of at most 0.0065.
Values may be sent and summed in bfloat16 or wider, within the bound.
A program may use at most 128 MiB of HBM per device.

v0:
```python
import jax
import jax.numpy as jnp
from jax import lax
from jax.sharding import PartitionSpec as P

HS = 16


def spatial_update(state_now, query_part, key_piece, value_piece, factor):
    heads_here = query_part.shape[2]
    size_head = query_part.shape[3]
    key_four = key_piece.reshape(key_piece.shape[0], key_piece.shape[1], heads_here, size_head)
    value_four = value_piece.reshape(
        value_piece.shape[0], value_piece.shape[1], heads_here, size_head
    )
    scores = (
        jnp.einsum("fqhd,fkhd->fhqk", query_part, key_four, preferred_element_type=jnp.float32)
        * factor
    )
    largest, total, accum = state_now
    new_largest = jnp.maximum(largest, jnp.max(scores, axis=-1))
    weights = jnp.exp(scores - new_largest[..., None])
    total = jnp.sum(weights, axis=-1)
    product = jnp.einsum(
        "fhqk,fkhd->fhqd",
        weights.astype(jnp.bfloat16),
        value_four,
        preferred_element_type=jnp.float32,
    )
    accum = product
    return (new_largest, total, accum)


def temporal_update(
    state_now, query_part, query_frames, key_piece, value_piece, key_frames, reach_heads, factor
):
    heads_here = query_part.shape[2]
    size_head = query_part.shape[3]
    key_four = key_piece.reshape(key_piece.shape[0], key_piece.shape[1], heads_here, size_head)
    value_four = value_piece.reshape(
        value_piece.shape[0], value_piece.shape[1], heads_here, size_head
    )
    scores = (
        jnp.einsum("fphd,gphd->phfg", query_part, key_four, preferred_element_type=jnp.float32)
        * factor
    )
    distance = jnp.abs(query_frames[:, None] - key_frames[None, :])
    allowed = (distance[None, :, :] <= reach_heads[:, None, None])[None]
    scores = jnp.where(allowed, scores, -1e30)
    largest, total, accum = state_now
    new_largest = jnp.maximum(largest, jnp.max(scores, axis=-1))
    weights = jnp.where(allowed, jnp.exp(scores - new_largest[..., None]), 0.0)
    total = jnp.sum(weights, axis=-1)
    product = jnp.einsum(
        "phfg,gphd->phfd",
        weights.astype(jnp.bfloat16),
        value_four,
        preferred_element_type=jnp.float32,
    )
    accum = product
    return (new_largest, total, accum)


def empty_state(lead_shape, size_head):
    return (
        jnp.full(lead_shape, -1e30, jnp.float32),
        jnp.zeros(lead_shape, jnp.float32),
        jnp.zeros(lead_shape + (size_head,), jnp.float32),
    )


def body(queries, keys, values, head_kind, frame_reach):
    frames_here, places, width = queries.shape
    heads_all = head_kind.shape[0]
    size_head = width // heads_all
    factor = size_head ** (-0.5)
    order = jnp.argsort(head_kind, stable=True)
    inverse = jnp.argsort(order)
    reach_time = jnp.take(frame_reach, order)[HS:]
    time_heads = heads_all - HS

    def arrange(tensor):
        return jnp.take(tensor.reshape(frames_here, places, heads_all, size_head), order, axis=2)

    query_heads = arrange(queries)
    key_heads = arrange(keys)
    value_heads = arrange(values)
    query_space = query_heads[:, :, :HS]
    key_space = key_heads[:, :, :HS].reshape(frames_here, places, HS * size_head)
    value_space = value_heads[:, :, :HS].reshape(frames_here, places, HS * size_head)
    query_time = query_heads[:, :, HS:]
    key_time = key_heads[:, :, HS:].reshape(frames_here, places, time_heads * size_head)
    value_time = value_heads[:, :, HS:].reshape(frames_here, places, time_heads * size_head)
    pieces = (
        lax.all_gather(key_space, "grp", axis=1, tiled=True),
        lax.all_gather(value_space, "grp", axis=1, tiled=True),
    )
    largest, total, accum = spatial_update(
        empty_state((frames_here, HS, places), size_head), query_space, pieces[0], pieces[1], factor
    )
    out_space = jnp.transpose(accum / total[..., None], (0, 2, 1, 3)).astype(jnp.bfloat16)
    query_frames = lax.axis_index("blk") * frames_here + jnp.arange(frames_here, dtype=jnp.int32)
    pieces = (
        lax.all_gather(key_time, "blk", axis=0, tiled=True),
        lax.all_gather(value_time, "blk", axis=0, tiled=True),
    )
    key_frames = jnp.arange(pieces[0].shape[0], dtype=jnp.int32)
    largest, total, accum = temporal_update(
        empty_state((places, time_heads, frames_here), size_head),
        query_time,
        query_frames,
        pieces[0],
        pieces[1],
        key_frames,
        reach_time,
        factor,
    )
    out_time = jnp.transpose(accum / total[..., None], (2, 0, 1, 3)).astype(jnp.bfloat16)
    joined = jnp.concatenate([out_space, out_time], axis=2)
    joined = jnp.take(joined, inverse, axis=2)
    return joined.reshape(frames_here, places, width)


def solution(mesh):
    placed = (P("blk", "grp", None), P("blk", "grp", None), P("blk", "grp", None), P(), P())
    return jax.shard_map(
        body, mesh=mesh, in_specs=placed, out_specs=P("blk", "grp", None), check_vma=False
    )
```

profile of v0, /device:TPU:0, one launch (start us, length us, event | category | flops | bytes accessed | tf_op | source)
XLA Modules:
  0.0 210.4 jit_solution(9516752081305793250)
XLA Ops:
  6.5 1.2 copy-done
  7.7 0.2 bitcast_bitcast_fusion
  7.9 2.3 %sort.34 = (s32[24]{0:T(128)}, s32[24]{0:T(128)S(1)}) sort(s32[24]{0:T(128)} %param.10, s32[24]{0:T(128)S(1)} %iota.14), dimensions={0}, to_apply=%region_0.0 | sort | flops 120 | bytes 384 | tf_op jit(solution)/shard_map/jit(argsort)/sort | solution.py:77
  10.2 1.6 gather_fusion.3
  11.8 0.7 gather_fusion
  12.6 1.4 bitcast_bitcast_fusion.1
  13.9 1.7 gather_fusion.2
  15.8 1.7 gather_fusion.1
  17.5 3.1 %bitcast_select_fusion.1 = (bf16[1,160,24,128]{3,1,2,0:T(8,128)(2,1)S(1)}, bf16[1,160,24,128]{3,1,2,0:T(8,128)(2,1)}, bf16[1,160,24,128]{3,1,2,0:T(8,128)(2,1)S(1)}) fusion(bf16[24,160,128]{2,1,0:T(8,128)(2,1)} %gather_fusion.3, pred[24]{0:T(512)(128)(4,1)S(1)} %get-tuple-element.11, bf16[24,160,128]{2,1,0:T(8,128)(2,1)} %gather_fusion.2, ...), kind=kLoop, calls=%fused_computation.24 | loop fusion | flops 1474560 | bytes 5898264 | tf_op jit(solution)/shard_map/jit(_take)/select_n | solution.py:83
  20.5 0.9 copy_bitcast_fusion.1
  21.5 2.0 copy_bitcast_fusion.2
  23.6 1.7 copy_bitcast_fusion.4
  25.5 0.8 copy_bitcast_fusion.3
  26.3 1.6 sort.35
  28.1 51.1 %all-gather.7.cloned.1.call-done = bf16[1,640,2048]{2,1,0:T(8,128)(2,1)} async-done(((bf16[1,160,2048]{2,1,0:T(8,128)(2,1)}), bf16[1,640,2048]{2,1,0:T(8,128)(2,1)}) %all-gather.7.cloned.1.call-update) | async-done | bytes 2621456 | tf_op jit(solution)/shard_map/all_gather | solution.py:96
  79.1 4.4 %copy.40 = bf16[1,640,2048]{1,2,0:T(8,128)(2,1)} copy(bf16[1,640,2048]{2,1,0:T(8,128)(2,1)} %all-gather.7.cloned.1.call-done) | data formatting | bytes 5242880 | tf_op jit(solution)/shard_map/all_gather | solution.py:96
  83.6 50.7 %all-gather.5.cloned.1.call-done = bf16[1,640,2048]{2,1,0:T(8,128)(2,1)} async-done(((bf16[1,160,2048]{2,1,0:T(8,128)(2,1)}), bf16[1,640,2048]{2,1,0:T(8,128)(2,1)}) %all-gather.5.cloned.1.call-update) | async-done | bytes 2621456 | tf_op jit(solution)/shard_map/all_gather | solution.py:95
  134.3 4.4 %copy.36 = bf16[1,640,2048]{1,2,0:T(8,128)(2,1)} copy(bf16[1,640,2048]{2,1,0:T(8,128)(2,1)} %all-gather.5.cloned.1.call-done) | data formatting | bytes 5242880 | tf_op jit(solution)/shard_map/all_gather | solution.py:95
  138.7 2.8 %multiply_reduce_fusion = (f32[16,160]{1,0:T(8,128)S(1)}, f32[16,160,640]{2,1,0:T(8,128)S(1)}) fusion(bf16[640,16,128]{0,2,1:T(8,128)(2,1)} %bitcast.116, bf16[1,160,24,128]{3,1,2,0:T(8,128)(2,1)S(1)} %get-tuple-element.16), kind=kOutput, calls=%fused_computation.6 | convolution fusion | flops 422704640 | bytes 9840640 | tf_op jit(solution)/shard_map/fqhd,fkhd->fhqk/dot_general | solution.py:17
  141.6 1.7 fusion
  143.4 1.9 fusion.13
  145.4 19.8 %all-gather.9.cloned.1.call-done = bf16[8,160,1024]{2,1,0:T(8,128)(2,1)} async-done(((bf16[1,160,1024]{2,1,0:T(8,128)(2,1)}), bf16[8,160,1024]{2,1,0:T(8,128)(2,1)}) %all-gather.9.cloned.1.call-update) | async-done | bytes 2621456 | tf_op jit(solution)/shard_map/all_gather | solution.py:104
  165.1 2.4 %copy.61 = bf16[160,8,8,128]{3,2,1,0:T(8,128)(2,1)S(1)} copy(bf16[160,8,8,128]{3,1,2,0:T(8,128)(2,1)} %bitcast.118) | data formatting | bytes 5242880
  167.5 2.0 fusion.8
  169.5 0.5 copy.49
  170.2 0.6 copy.50
  170.8 26.3 %all-gather.11.cloned.1.call-done = bf16[8,160,1024]{2,1,0:T(8,128)(2,1)} async-done(((bf16[1,160,1024]{2,1,0:T(8,128)(2,1)}), bf16[8,160,1024]{2,1,0:T(8,128)(2,1)}) %all-gather.11.cloned.1.call-update) | async-done | bytes 2621456 | tf_op jit(solution)/shard_map/all_gather | solution.py:105
  197.0 2.4 %copy.62 = bf16[160,8,8,128]{3,2,1,0:T(8,128)(2,1)S(1)} copy(bf16[160,8,8,128]{3,1,2,0:T(8,128)(2,1)} %bitcast.117) | data formatting | bytes 5242880
  199.4 2.1 %fusion.6 = f32[160,8,1,128]{3,2,1,0:T(1,128)S(1)} fusion(bf16[160,8,8,1]{2,3,1,0:T(2,128)(2,1)S(1)} %copy.50, bf16[8,160,8,128]{3,2,1,0:T(8,128)(2,1)S(1)} %bitcast.121), kind=kOutput, calls=%fused_computation.12 | convolution fusion | flops 2621440 | bytes 3297280 | tf_op jit(solution)/shard_map/phfg,gphd->phfd/dot_general | solution.py:54
  201.5 0.3 fusion.19
  201.9 0.7 gather_fusion.4
  202.7 1.2 copy_bitcast_fusion
  (33 shorter events, 1.0 us)
Async XLA Ops:
  6.5 1.2 copy-start
  6.5 5.3 %copy-start.1 = (s32[24]{0:T(128)S(1)}, s32[24]{0:T(128)}, u32[]{:S(2)}) copy-start(s32[24]{0:T(128)} %param.11) | copy-start | bytes 292
  6.5 72.6 %all-gather.7.cloned.1.call-start = ((), (), s32[]{:S(2)}) async-start(), calls=%async_computation.1 | async-start | bytes 3276800 | tf_op jit(solution)/shard_map/all_gather | solution.py:96
  11.8 3.8 %copy-start.3 = (bf16[1,160,3072]{2,1,0:T(8,128)(2,1)S(1)}, bf16[1,160,3072]{2,1,0:T(8,128)(2,1)}, u32[]{:S(2)}) copy-start(bf16[1,160,3072]{2,1,0:T(8,128)(2,1)} %param.7) | copy-start | bytes 2949124
  21.5 112.8 %all-gather.5.cloned.1.call-start = ((), (), s32[]{:S(2)}) async-start(), calls=%async_computation | async-start | bytes 3276800 | tf_op jit(solution)/shard_map/all_gather | solution.py:95
  23.6 141.5 %all-gather.9.cloned.1.call-start = ((), (), s32[]{:S(2)}) async-start(), calls=%async_computation.2 | async-start | bytes 2949120 | tf_op jit(solution)/shard_map/all_gather | solution.py:104
  25.4 171.6 %all-gather.11.cloned.1.call-start = ((), (), s32[]{:S(2)}) async-start(), calls=%async_computation.3 | async-start | bytes 2949120 | tf_op jit(solution)/shard_map/all_gather | solution.py:105
  141.6 1.8 copy-start.2
Sparse Core Ops, SparseCore 0:
  21.6 57.4 all-gather.6
  80.7 53.5 all-gather.4
  136.2 28.8 all-gather.8
  166.9 30.1 all-gather.10
where the time goes:
time: 211 us; the launch traced here: 210 us
  waiting for transfers between devices  148 us (70%)
  local copies, waits for them, and re-layouts  29.7 us (14%)
  between operations  13.3 us (6%)
  other arithmetic  10.5 us (5%)
  matrix products  8.86 us (4%)
    all_gather x1, waiting for transfers between devices, body(): lax.all_gather(value_space, 'grp', axis=1, tiled=True)  51.1 us
    all_gather x1, waiting for transfers between devices, body(): lax.all_gather(key_space, 'grp', axis=1, tiled=True)  50.7 us
    all_gather x1, waiting for transfers between devices, body(): lax.all_gather(value_time, 'blk', axis=0, tiled=True)  26.3 us
    all_gather x1, waiting for transfers between devices, body(): lax.all_gather(key_time, 'blk', axis=0, tiled=True)  19.8 us
    unnamed x10, local copies, waits for them, and re-layouts  6.11 us
    gather x3, local copies, waits for them, and re-layouts, arrange(): jnp.take(tensor.reshape(frames_here, places, heads_all, size_head), order...  5 us
    all_gather x1, local copies, waits for them, and re-layouts, body(): lax.all_gather(value_space, 'grp', axis=1, tiled=True)  4.43 us
    all_gather x1, local copies, waits for them, and re-layouts, body(): lax.all_gather(key_space, 'grp', axis=1, tiled=True)  4.42 us
  transfers between devices with their start and end apart: 4, of which 4 were waited for; matrix products, arithmetic and copies ran while one was open for 13% of the time, Pallas kernels for 0%

commit v1 on v0

v1 whole, which is shorter than its diff:
```python
import functools

import jax
import jax.numpy as jnp
from jax import lax
from jax.experimental import pallas as pl
from jax.experimental.pallas import tpu as pltpu
from jax.sharding import PartitionSpec as P

HS = 16
MESH = pl.DeviceIdType.MESH


def flip(me, other, size):
    total, place = 0, 1
    while place < size:
        mine = lax.rem(lax.div(me, jnp.int32(place)), jnp.int32(2))
        if isinstance(other, int):
            digit = (other // place) % 2
            changed = 1 - mine if digit else mine
        else:
            digit = lax.rem(lax.div(other, jnp.int32(place)), jnp.int32(2))
            changed = lax.rem(mine + digit, jnp.int32(2))
        total = total + place * changed
        place *= 2
    return total


def far_first(size):
    return [(step + size // 2) % size for step in range(size) if (step + size // 2) % size]


def weighted(q, k, v, factor, allowed=None):
    scores = lax.dot_general(q, k, (((1,), (1,)), ((), ())), preferred_element_type=jnp.float32)
    if allowed is not None:
        scores = jnp.where(allowed, scores, -1e30)
    top = jnp.max(scores, axis=-1, keepdims=True)
    weights = jnp.exp((scores - top) * factor)
    total = jnp.sum(weights, axis=-1, keepdims=True)
    summed = jnp.dot(weights.astype(jnp.bfloat16), v, preferred_element_type=jnp.float32)
    return (summed / total).astype(jnp.bfloat16)


def kernel(
    groups, frames,
    q_hbm, k_hbm, v_hbm, kind_ref, reach_ref, out_ref,
    stage, packed, packed_time, seen, seen_time, made, made_time, result, order, inverse,
    load_sem, space_send, space_recv, back_send, back_recv,
    time_send, time_recv, home_send, home_recv,
):
    heads = kind_ref.shape[0]
    places = stage.shape[2]
    size = stage.shape[3]
    owned = HS // groups
    splits = frames // (heads - HS)
    rows = places // splits
    factor = size ** (-0.5)
    me = lax.axis_index("grp")
    frame = lax.axis_index("blk")
    space_peers = far_first(groups)
    time_peers = far_first(frames)

    barrier = pltpu.get_barrier_semaphore()
    for d in space_peers:
        pl.semaphore_signal(
            barrier, inc=1, device_id={"grp": flip(me, d, groups)}, device_id_type=MESH
        )
    for d in time_peers:
        pl.semaphore_signal(
            barrier, inc=1, device_id={"blk": flip(frame, d, frames)}, device_id_type=MESH
        )
    loads = [
        pltpu.make_async_copy(
            source.at[:, h * size : (h + 1) * size], stage.at[part, h], load_sem.at[part, h]
        )
        for h in range(heads)
        for part, source in enumerate((q_hbm, k_hbm, v_hbm))
    ]
    for load in loads:
        load.start()

    near = jnp.int32(0)
    ends = []
    for h in range(heads):
        kind = kind_ref[h]
        inverse[h] = jnp.where(kind == 0, near, HS + h - near)
        near = near + (1 - kind)
        ends.append(near)

    def find(r, carry):
        first = jnp.int32(0)
        second = jnp.int32(0)
        for h in range(heads):
            first = first + jnp.where(ends[h] <= r, 1, 0)
            second = second + jnp.where(h + 1 - ends[h] <= r - HS, 1, 0)
        order[r] = jnp.minimum(jnp.where(r < HS, first, second), heads - 1)
        return carry

    lax.fori_loop(0, heads, find, 0)

    def space_copy(j, d):
        peer = flip(me, d, groups)
        return pltpu.make_async_remote_copy(
            src_ref=packed.at[peer * owned + j],
            dst_ref=seen.at[j, me],
            send_sem=space_send.at[j, d],
            recv_sem=space_recv.at[j, d],
            device_id={"grp": peer},
            device_id_type=MESH,
        )

    def back_copy(j, d):
        peer = flip(me, d, groups)
        return pltpu.make_async_remote_copy(
            src_ref=made.at[j, peer],
            dst_ref=result.at[me * owned + j],
            send_sem=back_send.at[j, d],
            recv_sem=back_recv.at[j, d],
            device_id={"grp": peer},
            device_id_type=MESH,
        )

    def rows_of(unit):
        if splits == 1:
            return pl.ds(0, rows)
        return pl.ds(pl.multiple_of(lax.rem(unit, jnp.int32(splits)) * rows, rows), rows)

    def time_copy(d):
        peer = flip(frame, d, frames)
        return pltpu.make_async_remote_copy(
            src_ref=packed_time.at[peer],
            dst_ref=seen_time.at[frame],
            send_sem=time_send.at[d],
            recv_sem=time_recv.at[d],
            device_id={"blk": peer},
            device_id_type=MESH,
        )

    def home_copy(d):
        peer = flip(frame, d, frames)
        return pltpu.make_async_remote_copy(
            src_ref=made_time.at[peer],
            dst_ref=result.at[HS + lax.div(frame, jnp.int32(splits)), rows_of(frame)],
            send_sem=home_send.at[d],
            recv_sem=home_recv.at[d],
            device_id={"blk": peer},
            device_id_type=MESH,
        )

    pl.semaphore_wait(barrier, len(space_peers) + len(time_peers))
    for load in loads:
        load.wait()

    def send_space(j):
        for d in space_peers:
            rank = flip(me, d, groups) * owned + j
            for part in range(3):
                packed[rank, part] = stage[part, order[rank]]
            space_copy(j, d).start()

    def pack_time(unit, target, slot):
        head = order[HS + lax.div(unit, jnp.int32(splits))]
        for part in range(3):
            target[slot, part] = stage[part, head, rows_of(unit)]

    send_space(0)
    for d in time_peers:
        peer = flip(frame, d, frames)
        pack_time(peer, packed_time, peer)
        time_copy(d).start()
    for j in range(1, owned):
        send_space(j)
    for j in range(owned):
        for part in range(3):
            seen[j, me, part] = stage[part, order[me * owned + j]]
    pack_time(frame, seen_time, frame)

    def space_head(j):
        for d in space_peers:
            space_copy(j, d).wait_recv()

        def block(step, carry):
            d = lax.rem(step + groups // 2, jnp.int32(groups))
            peer = flip(me, d, groups)
            made[j, peer] = weighted(
                seen[j, peer, 0],
                seen[j, :, 1].reshape(groups * places, size),
                seen[j, :, 2].reshape(groups * places, size),
                factor,
            )

            @pl.when(d != 0)
            def _():
                back_copy(j, d).start()

            return carry

        lax.fori_loop(0, groups, block, 0)
        result[me * owned + j] = made[j, me]

    def time_head():
        for d in time_peers:
            time_copy(d).wait_recv()
        reach = reach_ref[order[HS + lax.div(frame, jnp.int32(splits))]]
        wide = 256 // frames
        tokens = frames * wide
        left = lax.broadcasted_iota(jnp.int32, (tokens, tokens), 0)
        right = lax.broadcasted_iota(jnp.int32, (tokens, tokens), 1)
        log = wide.bit_length() - 1
        distance = jnp.abs((left >> log) - (right >> log))
        allowed = ((left & (wide - 1)) == (right & (wide - 1))) & (distance <= reach)

        def piece(at, carry):
            part_rows = pl.ds(pl.multiple_of(at * wide, wide), wide)
            q, k, v = (
                seen_time[:, part, part_rows].reshape(tokens, size) for part in range(3)
            )
            made_time[:, part_rows] = weighted(q, k, v, factor, allowed).reshape(
                frames, wide, size
            )
            return carry

        lax.fori_loop(0, rows // wide, piece, 0)
        for d in time_peers:
            home_copy(d).start()
        result[HS + lax.div(frame, jnp.int32(splits)), rows_of(frame)] = made_time[frame]

    def heads_loop(j, carry):
        space_head(j)
        return carry

    lax.fori_loop(0, 1, heads_loop, 0)
    time_head()
    lax.fori_loop(1, owned, heads_loop, 0)

    for d in time_peers:
        time_copy(d).wait_send()
        home_copy(d).wait()
    for j in range(owned):
        for d in space_peers:
            space_copy(j, d).wait_send()
            back_copy(j, d).wait()
    for h in range(heads):
        out_ref[:, h * size : (h + 1) * size] = result[inverse[h]]


def body(groups, frames, queries, keys, values, head_kind, frame_reach):
    frames_here, places, width = queries.shape
    heads = head_kind.shape[0]
    size = width // heads
    owned = HS // groups
    splits = frames // (heads - HS)
    assert frames_here == 1 and owned * groups == HS and splits * (heads - HS) == frames
    rows = places // splits
    bf16 = jnp.bfloat16
    out = pl.pallas_call(
        functools.partial(kernel, groups, frames),
        out_shape=jax.ShapeDtypeStruct((places, width), bf16),
        in_specs=[pl.BlockSpec(memory_space=pl.ANY)] * 3
        + [pl.BlockSpec(memory_space=pltpu.SMEM)] * 2,
        out_specs=pl.BlockSpec(memory_space=pltpu.VMEM),
        scratch_shapes=[
            pltpu.VMEM((3, heads, places, size), bf16),
            pltpu.VMEM((HS, 3, places, size), bf16),
            pltpu.VMEM((frames, 3, rows, size), bf16),
            pltpu.VMEM((owned, groups, 3, places, size), bf16),
            pltpu.VMEM((frames, 3, rows, size), bf16),
            pltpu.VMEM((owned, groups, places, size), bf16),
            pltpu.VMEM((frames, rows, size), bf16),
            pltpu.VMEM((heads, places, size), bf16),
            pltpu.SMEM((heads,), jnp.int32),
            pltpu.SMEM((heads,), jnp.int32),
            pltpu.SemaphoreType.DMA((3, heads)),
            pltpu.SemaphoreType.DMA((owned, groups)),
            pltpu.SemaphoreType.DMA((owned, groups)),
            pltpu.SemaphoreType.DMA((owned, groups)),
            pltpu.SemaphoreType.DMA((owned, groups)),
            pltpu.SemaphoreType.DMA((frames,)),
            pltpu.SemaphoreType.DMA((frames,)),
            pltpu.SemaphoreType.DMA((frames,)),
            pltpu.SemaphoreType.DMA((frames,)),
        ],
        compiler_params=pltpu.CompilerParams(
            collective_id=0, has_side_effects=True, vmem_limit_bytes=48 * 1024 * 1024
        ),
        name="exchange_attend",
    )(queries[0], keys[0], values[0], head_kind, frame_reach)
    return out[None]


def solution(mesh):
    placed = (P("blk", "grp", None), P("blk", "grp", None), P("blk", "grp", None), P(), P())
    return jax.shard_map(
        functools.partial(body, mesh.shape["grp"], mesh.shape["blk"]),
        mesh=mesh,
        in_specs=placed,
        out_specs=P("blk", "grp", None),
        check_vma=False,
    )
```

time: 211 us -> 71.4 us (0.34)
  waiting for transfers between devices: 148 us -> 0 us
  Pallas kernels: 0 us -> 65.9 us
  local copies, waits for them, and re-layouts: 29.7 us -> 5.22 us
  between operations: 13.3 us -> 0.01 us
  other arithmetic: 10.5 us -> 0 us
  matrix products: 8.86 us -> 0 us
    all_gather x4 -> x0, waiting for transfers between devices: 148 us -> none  [the longest x1 51.1 us: body(): lax.all_gather(value_space, 'grp', axis=1, tiled=True)]
    pallas_call x0 -> x1, Pallas kernels: none -> 65.9 us  [body(): pl.pallas_call(functools.partial(kernel, groups, frames), out_shape=jax.S...]
    dot_general x4 -> x0, matrix products: 8.86 us -> none  [the longest x1 2.85 us: spatial_update(): jnp.einsum('fqhd,fkhd->fhqk', query_part, key_four, preferred_element_typ...]
    all_gather x2 -> x0, local copies, waits for them, and re-layouts: 8.85 us -> none  [the longest x1 4.43 us: body(): lax.all_gather(value_space, 'grp', axis=1, tiled=True)]
    gather x5 -> x0, local copies, waits for them, and re-layouts: 6.43 us -> none  [the longest x3 5 us: arrange(): jnp.take(tensor.reshape(frames_here, places, heads_all, size_head), order...]
    reshape x4 -> x0, local copies, waits for them, and re-layouts: 5.47 us -> none  [the longest x1 2.04 us: body(): key_heads[:, :, :HS].reshape(frames_here, places, HS * size_head)]
    sort x2 -> x0, other arithmetic: 3.89 us -> none  [the longest x1 2.26 us: body(): order = jnp.argsort(head_kind, stable=True)]
    select_n x4 -> x0, other arithmetic: 3.08 us -> none  [the longest x2 3.06 us: arrange(): jnp.take(tensor.reshape(frames_here, places, heads_all, size_head), order...]
  transfers between devices with their start and end apart: 4 -> 0, of which waited for: 4 -> 0; matrix products, arithmetic and copies ran while one was open for 13% -> 0% of each run, Pallas kernels for 0% -> 0%
where the time goes in v1:
time: 71.4 us; the launch traced here: 71.1 us
  Pallas kernels  65.9 us (92%)
  local copies, waits for them, and re-layouts  5.22 us (7%)
    pallas_call x1, Pallas kernels, body(): pl.pallas_call(functools.partial(kernel, groups, frames), out_shape=jax.S...  65.9 us
    unnamed x11, local copies, waits for them, and re-layouts  5.22 us

profile of v1, /device:TPU:0, one launch (start us, length us, event | category | flops | bytes accessed | tf_op | source)
XLA Modules:
  0.0 71.1 jit_solution(4912224452799803359)
XLA Ops:
  0.0 0.0 copy-start.3
  0.0 0.0 copy-start.4
  0.0 0.7 copy-done.3
  0.7 0.0 copy-done.4
  0.7 0.0 copy-start
  0.7 1.2 %copy-done = bf16[1,160,3072]{2,1,0:T(8,128)(2,1)S(1)} copy-done((bf16[1,160,3072]{2,1,0:T(8,128)(2,1)S(1)}, bf16[1,160,3072]{2,1,0:T(8,128)(2,1)}, u32[]{:S(2)}) %copy-start) | copy-done | bytes 983064
  1.9 0.0 copy-start.1
  1.9 1.2 %copy-done.1 = bf16[1,160,3072]{2,1,0:T(8,128)(2,1)S(1)} copy-done((bf16[1,160,3072]{2,1,0:T(8,128)(2,1)S(1)}, bf16[1,160,3072]{2,1,0:T(8,128)(2,1)}, u32[]{:S(2)}) %copy-start.1) | copy-done | bytes 983064
  3.1 0.0 copy-start.2
  3.1 1.2 %copy-done.2 = bf16[1,160,3072]{2,1,0:T(8,128)(2,1)S(1)} copy-done((bf16[1,160,3072]{2,1,0:T(8,128)(2,1)S(1)}, bf16[1,160,3072]{2,1,0:T(8,128)(2,1)}, u32[]{:S(2)}) %copy-start.2) | copy-done | bytes 983064
  4.3 65.9 %exchange_attend.1 = bf16[160,3072]{1,0:T(8,128)(2,1)S(1)} custom-call(bf16[160,3072]{1,0:T(8,128)(2,1)S(1)} %bitcast.5, bf16[160,3072]{1,0:T(8,128)(2,1)S(1)} %bitcast.6, bf16[160,3072]{1,0:T(8,128)(2,1)S(1)} %bitcast.7, s32[24]{0:T(128)S(1)} %copy-done.3, s32[24]{0:T(128)S(1)} %copy-done.4), custom_call_target="tpu_custom_call" | custom-call | tf_op jit(solution)/shard_map/exchange_attend/pallas_call | solution.py:256
  70.2 0.9 %copy.7 = bf16[1,160,3072]{2,1,0:T(8,128)(2,1)} copy(bf16[1,160,3072]{2,1,0:T(8,128)(2,1)S(1)} %bitcast.4) | data formatting | bytes 1966080
Async XLA Ops:
  0.0 0.7 copy-start.3
  0.0 0.7 copy-start.4
  0.7 1.2 %copy-start = (bf16[1,160,3072]{2,1,0:T(8,128)(2,1)S(1)}, bf16[1,160,3072]{2,1,0:T(8,128)(2,1)}, u32[]{:S(2)}) copy-start(bf16[1,160,3072]{2,1,0:T(8,128)(2,1)} %param.5) | copy-start | bytes 2949124
  1.9 1.2 %copy-start.1 = (bf16[1,160,3072]{2,1,0:T(8,128)(2,1)S(1)}, bf16[1,160,3072]{2,1,0:T(8,128)(2,1)}, u32[]{:S(2)}) copy-start(bf16[1,160,3072]{2,1,0:T(8,128)(2,1)} %param.6) | copy-start | bytes 2949124
  3.1 1.2 %copy-start.2 = (bf16[1,160,3072]{2,1,0:T(8,128)(2,1)S(1)}, bf16[1,160,3072]{2,1,0:T(8,128)(2,1)}, u32[]{:S(2)}) copy-start(bf16[1,160,3072]{2,1,0:T(8,128)(2,1)} %param.7) | copy-start | bytes 2949124

commit v2 on v1

--- a/solution.py
+++ b/solution.py
@@ -43,9 +43,10 @@
 
 def kernel(
     groups, frames,
-    q_hbm, k_hbm, v_hbm, kind_ref, reach_ref, out_ref,
-    stage, packed, packed_time, seen, seen_time, made, made_time, result, order, inverse,
-    load_sem, space_send, space_recv, back_send, back_recv,
+    q_hbm, k_hbm, v_hbm, kind_hbm, reach_hbm, out_ref,
+    stage, packed, packed_time, seen, seen_time, made, made_time, result,
+    kind_ref, reach_ref, order, inverse, following,
+    small_sem, load_sem, space_send, space_recv, back_send, back_recv,
     time_send, time_recv, home_send, home_recv,
 ):
     heads = kind_ref.shape[0]
@@ -69,6 +70,12 @@
         pl.semaphore_signal(
             barrier, inc=1, device_id={"blk": flip(frame, d, frames)}, device_id_type=MESH
         )
+    smalls = [
+        pltpu.make_async_copy(kind_hbm, kind_ref, small_sem.at[0]),
+        pltpu.make_async_copy(reach_hbm, reach_ref, small_sem.at[1]),
+    ]
+    for small in smalls:
+        small.start()
     loads = [
         pltpu.make_async_copy(
             source.at[:, h * size : (h + 1) * size], stage.at[part, h], load_sem.at[part, h]
@@ -79,24 +86,27 @@
     for load in loads:
         load.start()
 
+    for small in smalls:
+        small.wait()
+
     near = jnp.int32(0)
-    ends = []
     for h in range(heads):
         kind = kind_ref[h]
         inverse[h] = jnp.where(kind == 0, near, HS + h - near)
         near = near + (1 - kind)
-        ends.append(near)
-
-    def find(r, carry):
-        first = jnp.int32(0)
-        second = jnp.int32(0)
-        for h in range(heads):
-            first = first + jnp.where(ends[h] <= r, 1, 0)
-            second = second + jnp.where(h + 1 - ends[h] <= r - HS, 1, 0)
-        order[r] = jnp.minimum(jnp.where(r < HS, first, second), heads - 1)
-        return carry
-
-    lax.fori_loop(0, heads, find, 0)
+    upcoming = [jnp.int32(heads - 1)] * 2
+    for h in range(heads, -1, -1):
+        if h < heads:
+            kind = kind_ref[h]
+            upcoming = [jnp.where(kind == want, h, upcoming[want]) for want in range(2)]
+        for want in range(2):
+            following[want, h] = upcoming[want]
+    for want, first, last in ((0, 0, HS), (1, HS, heads)):
+        head = following[want, 0]
+        for r in range(first, last):
+            order[r] = head
+            if r + 1 < last:
+                head = following[want, head + 1]
 
     def space_copy(j, d):
         peer = flip(me, d, groups)
@@ -256,8 +266,7 @@
     out = pl.pallas_call(
         functools.partial(kernel, groups, frames),
         out_shape=jax.ShapeDtypeStruct((places, width), bf16),
-        in_specs=[pl.BlockSpec(memory_space=pl.ANY)] * 3
-        + [pl.BlockSpec(memory_space=pltpu.SMEM)] * 2,
+        in_specs=[pl.BlockSpec(memory_space=pltpu.HBM)] * 5,
         out_specs=pl.BlockSpec(memory_space=pltpu.VMEM),
         scratch_shapes=[
             pltpu.VMEM((3, heads, places, size), bf16),
@@ -270,6 +279,10 @@
             pltpu.VMEM((heads, places, size), bf16),
             pltpu.SMEM((heads,), jnp.int32),
             pltpu.SMEM((heads,), jnp.int32),
+            pltpu.SMEM((heads,), jnp.int32),
+            pltpu.SMEM((heads,), jnp.int32),
+            pltpu.SMEM((2, heads + 1), jnp.int32),
+            pltpu.SemaphoreType.DMA((2,)),
             pltpu.SemaphoreType.DMA((3, heads)),
             pltpu.SemaphoreType.DMA((owned, groups)),
             pltpu.SemaphoreType.DMA((owned, groups)),
@@ -281,7 +294,7 @@
             pltpu.SemaphoreType.DMA((frames,)),
         ],
         compiler_params=pltpu.CompilerParams(
-            collective_id=0, has_side_effects=True, vmem_limit_bytes=48 * 1024 * 1024
+            collective_id=0, has_side_effects=True, vmem_limit_bytes=60 * 1024 * 1024
         ),
         name="exchange_attend",
     )(queries[0], keys[0], values[0], head_kind, frame_reach)

time: 71.4 us -> 68.7 us (0.962)
  local copies, waits for them, and re-layouts: 5.22 us -> 2.21 us
    unnamed x11 -> x1, local copies, waits for them, and re-layouts: 5.22 us -> 2.21 us
where the time goes in v2:
time: 68.7 us; the launch traced here: 68.5 us
  Pallas kernels  66.2 us (96%)
  local copies, waits for them, and re-layouts  2.21 us (3%)
    pallas_call x1, Pallas kernels, body(): pl.pallas_call(functools.partial(kernel, groups, frames), out_shape=jax.S...  66.2 us
    unnamed x1, local copies, waits for them, and re-layouts  2.21 us

profile of v2, /device:TPU:0, one launch (start us, length us, event | category | flops | bytes accessed | tf_op | source)
XLA Modules:
  0.0 68.5 jit_solution(13179796008369530443)
XLA Ops:
  0.0 66.2 %exchange_attend.1 = bf16[160,3072]{1,0:T(8,128)(2,1)} custom-call(bf16[160,3072]{1,0:T(8,128)(2,1)} %bitcast.5, bf16[160,3072]{1,0:T(8,128)(2,1)} %bitcast.6, bf16[160,3072]{1,0:T(8,128)(2,1)} %bitcast.7, s32[24]{0:T(128)} %kind_hbm.1, s32[24]{0:T(128)} %reach_hbm.1), custom_call_target="tpu_custom_call" | custom-call | tf_op jit(solution)/shard_map/exchange_attend/pallas_call | solution.py:266
  66.2 2.2 %copy.7 = bf16[1,160,3072]{2,1,0:T(8,128)(2,1)} copy(bf16[1,160,3072]{2,1,0:T(8,128)(2,1)} %bitcast.4) | data formatting | bytes 1966080

commit v3 on v2

--- a/solution.py
+++ b/solution.py
@@ -294,10 +294,15 @@
             pltpu.SemaphoreType.DMA((frames,)),
         ],
         compiler_params=pltpu.CompilerParams(
-            collective_id=0, has_side_effects=True, vmem_limit_bytes=60 * 1024 * 1024
+            collective_id=0, has_side_effects=True, vmem_limit_bytes=48 * 1024 * 1024
         ),
         name="exchange_attend",
-    )(queries[0], keys[0], values[0], head_kind, frame_reach)
+    )(
+        *(
+            pltpu.with_memory_space_constraint(operand, pltpu.HBM)
+            for operand in (queries[0], keys[0], values[0], head_kind, frame_reach)
+        )
+    )
     return out[None]
 
 

time: 68.7 us -> 66.4 us (0.967)
  local copies, waits for them, and re-layouts: 2.21 us -> 0.95 us
  Pallas kernels: 66.2 us -> 65.3 us
    unnamed x1, local copies, waits for them, and re-layouts: 2.21 us -> 0.95 us
    pallas_call x1, Pallas kernels: 66.2 us -> 65.3 us  [body(): pl.pallas_call(functools.partial(kernel, groups, frames), out_shape=jax.S...]
where the time goes in v3:
time: 66.4 us; the launch traced here: 66.2 us
  Pallas kernels  65.3 us (98%)
  local copies, waits for them, and re-layouts  0.95 us (1%)
    pallas_call x1, Pallas kernels, body(): pl.pallas_call(functools.partial(kernel, groups, frames), out_shape=jax.S...  65.3 us

profile of v3, /device:TPU:0, one launch (start us, length us, event | category | flops | bytes accessed | tf_op | source)
XLA Modules:
  0.0 66.2 jit_solution(13540863490066959572)
XLA Ops:
  0.0 65.3 %exchange_attend.1 = bf16[160,3072]{1,0:T(8,128)(2,1)S(1)} custom-call(bf16[160,3072]{1,0:T(8,128)(2,1)} %bitcast.5, bf16[160,3072]{1,0:T(8,128)(2,1)} %bitcast.6, bf16[160,3072]{1,0:T(8,128)(2,1)} %bitcast.7, s32[24]{0:T(128)} %kind_hbm.1, s32[24]{0:T(128)} %reach_hbm.1), custom_call_target="tpu_custom_call" | custom-call | tf_op jit(solution)/shard_map/exchange_attend/pallas_call | solution.py:266
  65.3 0.9 %copy.7 = bf16[1,160,3072]{2,1,0:T(8,128)(2,1)} copy(bf16[1,160,3072]{2,1,0:T(8,128)(2,1)S(1)} %bitcast.4) | data formatting | bytes 1966080

commit v4 on v3

--- a/solution.py
+++ b/solution.py
@@ -44,14 +44,15 @@
 def kernel(
     groups, frames,
     q_hbm, k_hbm, v_hbm, kind_hbm, reach_hbm, out_ref,
-    stage, packed, packed_time, seen, seen_time, made, made_time, result,
+    stage_q, stage_k, stage_v, packed, packed_time, seen, seen_time, made, made_time, result,
     kind_ref, reach_ref, order, inverse, following,
-    small_sem, load_sem, space_send, space_recv, back_send, back_recv,
+    small_sem, load_sem, first_send, first_recv, space_send, space_recv, back_send, back_recv,
     time_send, time_recv, home_send, home_recv,
 ):
     heads = kind_ref.shape[0]
-    places = stage.shape[2]
-    size = stage.shape[3]
+    stage = (stage_q, stage_k, stage_v)
+    places = stage_q.shape[1]
+    size = stage_q.shape[2]
     owned = HS // groups
     splits = frames // (heads - HS)
     rows = places // splits
@@ -78,10 +79,10 @@
         small.start()
     loads = [
         pltpu.make_async_copy(
-            source.at[:, h * size : (h + 1) * size], stage.at[part, h], load_sem.at[part, h]
-        )
+            source.at[:, h * size : (h + 1) * size], stage[part].at[h], load_sem.at[part, h]
+        )
+        for part, source in enumerate((q_hbm, k_hbm, v_hbm))
         for h in range(heads)
-        for part, source in enumerate((q_hbm, k_hbm, v_hbm))
     ]
     for load in loads:
         load.start()
@@ -119,6 +120,17 @@
             device_id_type=MESH,
         )
 
+    def first_copy(part, d):
+        peer = flip(me, d, groups)
+        return pltpu.make_async_remote_copy(
+            src_ref=packed.at[peer * owned, part],
+            dst_ref=seen.at[0, me, part],
+            send_sem=first_send.at[part, d],
+            recv_sem=first_recv.at[part, d],
+            device_id={"grp": peer},
+            device_id_type=MESH,
+        )
+
     def back_copy(j, d):
         peer = flip(me, d, groups)
         return pltpu.make_async_remote_copy(
@@ -158,22 +170,26 @@
         )
 
     pl.semaphore_wait(barrier, len(space_peers) + len(time_peers))
-    for load in loads:
-        load.wait()
 
     def send_space(j):
         for d in space_peers:
             rank = flip(me, d, groups) * owned + j
             for part in range(3):
-                packed[rank, part] = stage[part, order[rank]]
+                packed[rank, part] = stage[part][order[rank]]
             space_copy(j, d).start()
 
     def pack_time(unit, target, slot):
         head = order[HS + lax.div(unit, jnp.int32(splits))]
         for part in range(3):
-            target[slot, part] = stage[part, head, rows_of(unit)]
-
-    send_space(0)
+            target[slot, part] = stage[part][head, rows_of(unit)]
+
+    for part in range(3):
+        for load in loads[part * heads : (part + 1) * heads]:
+            load.wait()
+        for d in space_peers:
+            rank = flip(me, d, groups) * owned
+            packed[rank, part] = stage[part][order[rank]]
+            first_copy(part, d).start()
     for d in time_peers:
         peer = flip(frame, d, frames)
         pack_time(peer, packed_time, peer)
@@ -182,13 +198,10 @@
         send_space(j)
     for j in range(owned):
         for part in range(3):
-            seen[j, me, part] = stage[part, order[me * owned + j]]
+            seen[j, me, part] = stage[part][order[me * owned + j]]
     pack_time(frame, seen_time, frame)
 
     def space_head(j):
-        for d in space_peers:
-            space_copy(j, d).wait_recv()
-
         def block(step, carry):
             d = lax.rem(step + groups // 2, jnp.int32(groups))
             peer = flip(me, d, groups)
@@ -236,19 +249,28 @@
         result[HS + lax.div(frame, jnp.int32(splits)), rows_of(frame)] = made_time[frame]
 
     def heads_loop(j, carry):
+        for d in space_peers:
+            space_copy(j, d).wait_recv()
         space_head(j)
         return carry
 
-    lax.fori_loop(0, 1, heads_loop, 0)
+    for d in space_peers:
+        for part in range(3):
+            first_copy(part, d).wait_recv()
+    space_head(0)
     time_head()
     lax.fori_loop(1, owned, heads_loop, 0)
 
     for d in time_peers:
         time_copy(d).wait_send()
         home_copy(d).wait()
+    for d in space_peers:
+        for part in range(3):
+            first_copy(part, d).wait_send()
     for j in range(owned):
         for d in space_peers:
-            space_copy(j, d).wait_send()
+            if j > 0:
+                space_copy(j, d).wait_send()
             back_copy(j, d).wait()
     for h in range(heads):
         out_ref[:, h * size : (h + 1) * size] = result[inverse[h]]
@@ -269,7 +291,9 @@
         in_specs=[pl.BlockSpec(memory_space=pltpu.HBM)] * 5,
         out_specs=pl.BlockSpec(memory_space=pltpu.VMEM),
         scratch_shapes=[
-            pltpu.VMEM((3, heads, places, size), bf16),
+            pltpu.VMEM((heads, places, size), bf16),
+            pltpu.VMEM((heads, places, size), bf16),
+            pltpu.VMEM((heads, places, size), bf16),
             pltpu.VMEM((HS, 3, places, size), bf16),
             pltpu.VMEM((frames, 3, rows, size), bf16),
             pltpu.VMEM((owned, groups, 3, places, size), bf16),
@@ -284,6 +308,8 @@
             pltpu.SMEM((2, heads + 1), jnp.int32),
             pltpu.SemaphoreType.DMA((2,)),
             pltpu.SemaphoreType.DMA((3, heads)),
+            pltpu.SemaphoreType.DMA((3, groups)),
+            pltpu.SemaphoreType.DMA((3, groups)),
             pltpu.SemaphoreType.DMA((owned, groups)),
             pltpu.SemaphoreType.DMA((owned, groups)),
             pltpu.SemaphoreType.DMA((owned, groups)),

time: 66.4 us -> 66.5 us (level)
  no operation moved by 1% of the time
where the time goes in v4:
time: 66.5 us; the launch traced here: 66.3 us
  Pallas kernels  65.4 us (98%)
  local copies, waits for them, and re-layouts  0.95 us (1%)
    pallas_call x1, Pallas kernels, body(): pl.pallas_call(functools.partial(kernel, groups, frames), out_shape=jax.S...  65.4 us

profile of v4, /device:TPU:0, one launch (start us, length us, event | category | flops | bytes accessed | tf_op | source)
XLA Modules:
  0.0 66.3 jit_solution(14647276580545333595)
XLA Ops:
  0.0 65.4 %exchange_attend.1 = bf16[160,3072]{1,0:T(8,128)(2,1)S(1)} custom-call(bf16[160,3072]{1,0:T(8,128)(2,1)} %bitcast.5, bf16[160,3072]{1,0:T(8,128)(2,1)} %bitcast.6, bf16[160,3072]{1,0:T(8,128)(2,1)} %bitcast.7, s32[24]{0:T(128)} %kind_hbm.1, s32[24]{0:T(128)} %reach_hbm.1), custom_call_target="tpu_custom_call" | custom-call | tf_op jit(solution)/shard_map/exchange_attend/pallas_call | solution.py:288
  65.4 0.9 %copy.7 = bf16[1,160,3072]{2,1,0:T(8,128)(2,1)} copy(bf16[1,160,3072]{2,1,0:T(8,128)(2,1)S(1)} %bitcast.4) | data formatting | bytes 1966080
